TPU v7x, 32 devices: a whole 2x2x4 slice. The times are simulated.
32 devices in a mesh: img: 8 (over y, x, core), row: 4 (over z).
Axes of the slice: x: 2, y: 2, z: 4, core: 2. Of those that a mesh axis runs over, the one named last changes fastest.
Arguments:
- latents: bfloat16 [64, 512, 1024], P('img', 'row'), may hold values from -6 to 6
- cotangent: bfloat16 [64, 512, 1024], P('img', 'row'), may hold values from -6 to 6
- slot_crops: int32 [64], P('img'), may hold values from 0 to 8, as said below
- ln1_scale: bfloat16 [1024], replicated, may hold values from 0.25 to 1.75
- ln1_offset: bfloat16 [1024], replicated, may hold values from -1.5 to 1.5
- qkv_weight: bfloat16 [1024, 3072], replicated, may hold values from -0.25 to 0.25
- out_weight: bfloat16 [1024, 1024], replicated, may hold values from -0.5 to 0.5
- out_bias: bfloat16 [1024], replicated, may hold values from -1.5 to 1.5
- ln2_scale: bfloat16 [1024], replicated, may hold values from 0.25 to 1.75
- ln2_offset: bfloat16 [1024], replicated, may hold values from -1.5 to 1.5
- up_weight: bfloat16 [1024, 1024], replicated, may hold values from -0.1875 to 0.1875
- up_bias: bfloat16 [1024], replicated, may hold values from -2.5 to 2.5
- down_weight: bfloat16 [1024, 1024], replicated, may hold values from -0.25 to 0.25
- down_bias: bfloat16 [1024], replicated, may hold values from -1.5 to 1.5
Outputs:
- block_out: bfloat16 [64, 512, 1024], P('img', 'row')
- latents_grad: bfloat16 [64, 512, 1024], P('img', 'row')
- ln1_scale_grad: float32 [1024], P(('img', 'row'))
- ln1_offset_grad: float32 [1024], P(('img', 'row'))
- qkv_weight_grad: float32 [1024, 3072], P(('img', 'row'))
- out_weight_grad: float32 [1024, 1024], P(('img', 'row'))
- out_bias_grad: float32 [1024], P(('img', 'row'))
- ln2_scale_grad: float32 [1024], P(('img', 'row'))
- ln2_offset_grad: float32 [1024], P(('img', 'row'))
- up_weight_grad: float32 [1024, 1024], P(('img', 'row'))
- up_bias_grad: float32 [1024], P(('img', 'row'))
- down_weight_grad: float32 [1024, 1024], P(('img', 'row'))
- down_bias_grad: float32 [1024], P(('img', 'row'))
Inputs may be any that keep to these rules, and one draw needn't show every extreme that they name: `slot_crops`: A slot holds the number of crops of its image, 1 to 8, or 0 if it is empty. The full slots, in slot order, hold the images one after another, each image's crops in consecutive full slots; the first image has 8 crops in every draw. Each index of img holds at least one full slot, its empty slots stand after its full ones, the first index of img has no empty slot and the last at least one.
All inputs are finite; a program needn't handle non-finite values.
Results may differ from a plain program's by a relative error of at most 0.015.
Values may be sent and summed in bfloat16 or wider, within the bound.
A program may use at most 256 MiB of HBM per device.

v0:
```python
import functools
import jax
import jax.numpy as jnp
from jax import lax
from jax.experimental import pallas as pl
from jax.experimental.pallas import tpu as pltpu
from jax.sharding import PartitionSpec as P

HEADS = 8
EPSILON = 1e-05
F32 = jnp.float32
BF16 = jnp.bfloat16
MESH = pl.DeviceIdType.MESH
ANY = pl.BlockSpec(memory_space=pl.ANY)
VM = pl.BlockSpec(memory_space=pltpu.VMEM)
SM = pl.BlockSpec(memory_space=pltpu.SMEM)
GELU_A = 0.7978845608028654
GELU_B = 0.044715
LOG2_E = 1.4426950408889634
VMEM_LIMIT = 64 * 1024 * 1024 - 64 * 1024


def dot(a, b):
    return jnp.dot(a, b, preferred_element_type=F32)


def dot_t(a, b):
    return lax.dot_general(a, b, (((1,), (1,)), ((), ())), preferred_element_type=F32)


def dot_tt(a, b):
    return lax.dot_general(a, b, (((0,), (0,)), ((), ())), preferred_element_type=F32)


def norm_parts(values):
    mean = jnp.mean(values, -1, keepdims=True)
    centred = values - mean
    inverse = lax.rsqrt(jnp.mean(centred * centred, -1, keepdims=True) + EPSILON)
    return centred * inverse, inverse


def norm_back(scaled, hat, inverse):
    return inverse * (scaled - jnp.mean(scaled, -1, keepdims=True) - hat * jnp.mean(scaled * hat, -1, keepdims=True))


def column_sum(values):
    return jnp.sum(values, 0, keepdims=True)


def bits_of(extent):
    return [1 << i for i in range(extent.bit_length() - 1)]


def flipped(index, bit):
    return index + bit - 2 * bit * ((index // bit) % 2)


def block_kernel(images, lanes, places, steps_left, steps_right, in_lanes, *refs):
    crops, vectors, (lat, cot), refs = refs[0], refs[1:8], refs[8:10], refs[10:]
    mats, refs = refs[:4], refs[4:]
    (out_block, out_grad), refs = refs[:2], refs[2:]
    mlp_out, (qkv_out, sums_out), refs = refs[:3], refs[3:5], refs[5:]
    (vq, vo, vu, vd, xr, cr, h1, qkv, resid, work, back, gm, bo, lse, sums, sums_got, got_first, got_next), refs = refs[:18], refs[18:]
    (mat_sem, own_sem, lat_out, lat_in, cot_out, cot_in, bo_out, bo_in, lg_out, lg_in,
     red_out, red_in, credit, sum_out, sum_in) = refs
    rounds, rows, width = h1.shape
    chunk = rows // lanes
    size = width // HEADS
    img, z = lax.axis_index("img"), lax.axis_index("row")
    left_pages, slope = 6, 0
    act, h2, mixed = (left_pages + rounds * i for i in range(3))
    gl, gp, ga = (rounds * i for i in range(3))
    last = rounds - 1

    def device(axis, bit):
        return (flipped(img, bit), z) if axis == "img" else (img, flipped(z, bit))

    def lane(k):
        other = z
        for bit in bits_of(lanes):
            if k & bit:
                other = flipped(other, bit)
        return other

    def place(r, other):
        return r * lanes + other

    def loop_rounds(body):
        pl.loop(0, rounds)(body)

    partners = {(axis, bit) for axis, bit in steps_left} | {("row", bit) for bit in bits_of(lanes)}
    friends = [device(axis, bit) for axis, bit in sorted(partners)]
    friends += [(img, lane(k)) for k in range(1, lanes) if k & (k - 1)]
    barrier = pltpu.get_barrier_semaphore()
    for friend in friends:
        pl.semaphore_signal(barrier, inc=1, device_id=friend, device_id_type=MESH)
    loads = [pltpu.make_async_copy(a, b, mat_sem.at[i]) for i, (a, b) in enumerate(zip(mats, (vq, vo, vu, vd)))]

    def piece_in(source, target, sent, got, own, r, k):
        if k == 0:
            return pltpu.make_async_copy(source.at[place(r, z)], target.at[r, pl.ds(0, chunk)], own_sem.at[own, r])
        return pltpu.make_async_remote_copy(
            src_ref=source.at[place(r, lane(k))], dst_ref=target.at[r, pl.ds(k * chunk, chunk)],
            send_sem=sent.at[r, k], recv_sem=got.at[r, k], device_id=(img, lane(k)), device_id_type=MESH)

    def piece_out(source, target, sent, got, own, r, k):
        if k == 0:
            return pltpu.make_async_copy(source.at[r, pl.ds(0, chunk)], target.at[place(r, z)], own_sem.at[own, r])
        return pltpu.make_async_remote_copy(
            src_ref=source.at[r, pl.ds(k * chunk, chunk)], dst_ref=target.at[place(r, z)],
            send_sem=sent.at[r, k], recv_sem=got.at[r, k], device_id=(img, lane(k)), device_id_type=MESH)

    lat_piece = functools.partial(piece_in, lat, xr, lat_out, lat_in, 0)
    cot_piece = functools.partial(piece_in, cot, cr, cot_out, cot_in, 1)
    bo_piece = functools.partial(piece_out, bo, out_block, bo_out, bo_in, 2)
    lg_piece = functools.partial(piece_out, xr, out_grad, lg_out, lg_in, 3)

    def arrive(piece, r, k):
        move = piece(r, k)
        move.wait() if k == 0 else move.wait_recv()

    for load in loads:
        load.start()
    for piece in (lat_piece, cot_piece):
        for r in range(rounds):
            piece(r, 0).start()
    sums[...] = jnp.zeros_like(sums)
    pl.semaphore_wait(barrier, len(friends))

    def issue(piece, r):
        for k in range(lanes - 1, 0, -1):
            piece(r, k).start()

    issue(lat_piece, 0)

    half = rows // 2
    halves = [pl.ds(i * half, half) for i in range(2)]
    vector = lambda i: vectors[i][...].astype(F32).reshape(1, width)

    def head_columns(h):
        return pl.ds(pl.multiple_of(h * size, size), size)

    def forward(r):
        s1, o1 = vector(0), vector(1)
        for k in range(lanes):
            arrive(lat_piece, r, k)
            part = pl.ds(k * chunk, chunk)
            hat, _ = norm_parts(xr[r, part, :].astype(F32))
            h1[r, part, :] = (hat * s1 + o1).astype(BF16)

        @pl.when(r < last)
        def _():
            issue(lat_piece, r + 1)

        @pl.when(r == last)
        def _():
            issue(cot_piece, 0)

        for n in range(3):
            qkv[3 * r + n] = dot(h1[r], vq[:, n * width:(n + 1) * width]).astype(BF16)
        factor = size ** -0.5 * LOG2_E

        @pl.loop(0, HEADS // 4)
        def _(group):
            for i in range(4):
                cols = head_columns(4 * group + i)
                q, k, v = qkv[3 * r, :, cols], qkv[3 * r + 1, :, cols], qkv[3 * r + 2, :, cols]
                s = dot_t(q, k)
                top = jnp.max(s, 1, keepdims=True)
                e = jnp.exp2((s - top) * factor)
                total = jnp.sum(e, 1, keepdims=True)
                lse[r, group, :, i:i + 1] = top * factor + jnp.log2(total)
                work[mixed + r, :, cols] = (dot(e.astype(BF16), v) * (1.0 / total)).astype(BF16)

        bo_, s2, o2 = vector(4), vector(2), vector(3)
        for part in halves:
            value = xr[r, part, :].astype(F32) + dot(work[mixed + r, part, :], vo[...]) + bo_
            resid[r, part, :] = value
            hat, _ = norm_parts(value)
            work[h2 + r, part, :] = (hat * s2 + o2).astype(BF16)
        bu = vector(5)
        for part in halves:
            u = dot(work[h2 + r, part, :], vu[...]) + bu
            t = jnp.tanh(GELU_A * (u + GELU_B * u * u * u))
            work[act + r, part, :] = (0.5 * u * (1.0 + t)).astype(BF16)
            work[slope + r, part, :] = (
                0.5 * (1.0 + t) + 0.5 * u * (1.0 - t * t) * (GELU_A * (1.0 + 3.0 * GELU_B * u * u))
            ).astype(BF16)
        bd = vector(6)
        keep = jnp.minimum(crops[place(r, z)], 1).astype(F32)
        for part in halves:
            value = resid[r, part, :] + dot(work[act + r, part, :], vd[...]) + bd
            bo[r, part, :] = (value * keep).astype(BF16)
        bo_piece(r, 0).start()

    def add_sum(index, value):
        sums[0, index:index + 1, :] = sums[0, index:index + 1, :] + value

    def backward_mlp(r):
        held = crops[place(r, z)]
        share = jnp.full((1, width), jnp.minimum(held, 1).astype(F32)) / jnp.full((1, width), jnp.maximum(held, 1).astype(F32))
        for k in range(lanes):
            arrive(cot_piece, r, k)
            part = pl.ds(k * chunk, chunk)
            g = (cr[r, part, :].astype(F32) * share).astype(BF16)
            back[gl + r, part, :] = g
            add_sum(0, column_sum(g.astype(F32)))

        @pl.when(r < last)
        def _():
            issue(cot_piece, r + 1)

        @pl.when(r == last)
        def _():
            for s in range(rounds):
                issue(bo_piece, s)

        for part in halves:
            g = (dot_t(back[gl + r, part, :], vd[...]) * work[slope + r, part, :].astype(F32)).astype(BF16)
            back[gp + r, part, :] = g
            add_sum(1, column_sum(g.astype(F32)))
        s2 = vector(2)
        for part in halves:
            gh = dot_t(back[gp + r, part, :], vu[...])
            hat, inverse = norm_parts(resid[r, part, :])
            add_sum(2, column_sum(gh * hat))
            add_sum(3, column_sum(gh))
            value = cr[r, part, :].astype(F32) * share + norm_back(gh * s2, hat, inverse)
            resid[r, part, :] = value
            g = value.astype(BF16)
            back[ga + r, part, :] = g
            add_sum(4, column_sum(g.astype(F32)))
        for part in halves:
            gm[0, part, :] = dot_t(back[ga + r, part, :], vo[...]).astype(BF16)

    def backward_attention(r):
        factor = size ** -0.5

        for h in range(HEADS):
            if h % 4 == 0:
                lse_rows = lse[r, h // 4].T
            cols = slice(h * size, (h + 1) * size)
            q, k, v, m = qkv[3 * r, :, cols], qkv[3 * r + 1, :, cols], qkv[3 * r + 2, :, cols], gm[0, :, cols]
            p = jnp.exp2(dot_t(k, q) * (factor * LOG2_E) - lse_rows[h % 4:h % 4 + 1, :])
            dp = dot_t(v, m)
            ds = (p * (dp - jnp.sum(p * dp, 0, keepdims=True))).astype(BF16)
            qkv[3 * r + 2, :, cols] = dot(p.astype(BF16), m).astype(BF16)
            qkv[3 * r + 1, :, cols] = (dot(ds, q) * factor).astype(BF16)
            qkv[3 * r, :, cols] = (dot(k.T, ds) * factor).T.astype(BF16)

    def backward_input(r):
        s1 = vector(0)
        for part in halves:
            gh = dot_t(qkv[3 * r, part, :], vq[:, :width])
            gh = gh + dot_t(qkv[3 * r + 1, part, :], vq[:, width:2 * width])
            gh = gh + dot_t(qkv[3 * r + 2, part, :], vq[:, 2 * width:])
            hat, inverse = norm_parts(xr[r, part, :].astype(F32))
            add_sum(5, column_sum(gh * hat))
            add_sum(6, column_sum(gh))
            xr[r, part, :] = (resid[r, part, :] + norm_back(gh * s1, hat, inverse)).astype(BF16)

    count = len(steps_left)
    unit = width >> count
    per_half = width // 2 // unit
    sides = (slice(0, width // 2), slice(width // 2, width))

    def spot(block, steps):
        found = 0
        for axis, bit in steps:
            mine = (img // bit) % 2 if axis == "img" else (z // bit) % 2
            scale = 1 if axis == "row" else (width // unit) // images
            theirs = (block // (bit * scale)) % 2
            found = found * 2 + (theirs + mine) % 2
        return found

    def place_products(base, left, right):
        @pl.loop(0, 3)
        def _(c):
            for steps, offset in ((steps_left, 0), (steps_right, width // 2)):
                for first_column in range(offset, offset + width // 2, 256):
                    cols = slice(first_column, first_column + 256)
                    total = dot_tt(left(c, 0), right(c, 0, cols))
                    for r in range(1, rounds):
                        total = total + dot_tt(left(c, r), right(c, r, cols))
                    total = total.astype(BF16)
                    for block in range(width // unit):
                        at = spot(block, steps)
                        first = pl.multiple_of((at % per_half) * unit, unit)
                        work[base + c + 3 * (at // per_half), pl.ds(first, unit), cols] = total[block * unit:(block + 1) * unit]

    def send(base, group, step, side):
        steps = (steps_left, steps_right)[side]
        if step == 0:
            source, target = work.at[pl.ds(base + 3, 3)], got_first
        else:
            length = rows >> step
            source = work.at[pl.ds(base, 3), pl.ds(length, length), sides[side]]
            target = got_next.at[:, pl.ds(rows - 2 * length, length), sides[side]]
        return pltpu.make_async_remote_copy(
            src_ref=source, dst_ref=target, send_sem=red_out.at[group, step, side], recv_sem=red_in.at[group, step, side],
            device_id=device(*steps[step]), device_id_type=MESH)

    def begin(base, group, step, side):
        if group:
            pl.semaphore_wait(credit.at[step, side], 1)
        send(base, group, step, side).start()

    def reduce_step(base, group, step):
        length = rows >> step
        middle = length // 2
        for side in (0, 1):
            cols = sides[side]
            if step or side == 0:
                send(base, group, step, side).wait_recv()

            def added(c, first, extent):
                if step == 0:
                    got = got_first[c, pl.ds(first, extent), cols]
                else:
                    got = got_next[c, pl.ds(rows - 2 * length + first, extent), cols]
                return work[base + c, pl.ds(first, extent), cols].astype(F32) + got.astype(F32)

            if step == count - 1:
                for c in range(3):
                    if group:
                        qkv_out[:, c * width + cols.start:c * width + cols.stop] = added(c, 0, length)
                    else:
                        mlp_out[c][:, cols] = added(c, 0, length)
            else:
                def keep_part(first):
                    @pl.loop(0, 3)
                    def _(c):
                        work[base + c, pl.ds(first, middle), cols] = added(c, first, middle).astype(BF16)

                keep_part(middle)
                begin(base, group, step + 1, side)
                keep_part(0)
            if group == 0 and (step or side):
                steps = (steps_left, steps_right)[side]
                pl.semaphore_signal(
                    credit.at[step, side if step else 0], inc=1, device_id=device(*steps[step]), device_id_type=MESH)

    mlp_base, qkv_base = 0, left_pages
    for load in loads:
        load.wait()
    loop_rounds(forward)

    @loop_rounds
    def _(r):
        backward_mlp(r)

        @pl.when(r == last)
        def _():
            place_products(
                mlp_base, lambda c, s: work[left_pages + rounds * c + s], lambda c, s, cols: back[rounds * c + s, :, cols])
            begin(mlp_base, 0, 0, 0)

        backward_attention(r)

        @pl.when(r == last)
        def _():
            for s in range(last):
                issue(lg_piece, s)
            reduce_step(mlp_base, 0, 0)
            place_products(qkv_base, lambda c, s: h1[s], lambda c, s, cols: qkv[3 * s + c, :, cols])
            begin(qkv_base, 1, 0, 0)

        backward_input(r)
        lg_piece(r, 0).start()


    gates = {count - 3: [2], count - 2: [3], count - 1: [1]} if in_lanes and lanes == 4 else {0: range(1, lanes)}

    def results_out(step):
        for k in gates.get(step, ()):
            lg_piece(last, k).start()

    sum_moves = [
        pltpu.make_async_remote_copy(
            src_ref=sums.at[i], dst_ref=sums_got.at[i], send_sem=sum_out.at[i], recv_sem=sum_in.at[i],
            device_id=device(axis, bit), device_id_type=MESH)
        for i, (axis, bit) in enumerate(steps_left)
    ]
    sum_moves[0].start()
    results_out(0)
    for step in range(1, count + 1):
        if step < count:
            reduce_step(mlp_base, 0, step)
        if step == count - 3:
            results_out(step)
        reduce_step(qkv_base, 1, step - 1)
        if step > count - 3:
            results_out(step)
        sum_moves[step - 1].wait()
        sums[step] = sums[step - 1] + sums_got[step - 1]
        if step < count:
            sum_moves[step].start()
    sums_out[...] = sums[count]

    for group, base in enumerate((mlp_base, qkv_base)):
        send(base, group, 0, 0).wait_send()
        for step in range(1, count):
            for side in (0, 1):
                send(base, group, step, side).wait_send()
    for r in range(rounds):
        for k in range(1, lanes):
            lat_piece(r, k).wait_send()
            cot_piece(r, k).wait_send()
        for piece in (bo_piece, lg_piece):
            for k in range(lanes):
                piece(r, k).wait()


def local(
    latents, cotangent, slot_crops, ln1_scale, ln1_offset, qkv_weight, out_weight, out_bias,
    ln2_scale, ln2_offset, up_weight, up_bias, down_weight, down_bias,
):
    slots, chunk, width = latents.shape
    images, lanes = lax.axis_size("img"), lax.axis_size("row")
    rounds = slots // lanes
    rows = chunk * lanes
    devices = images * lanes
    image_bits = bits_of(images)
    left = [("img", image_bits[0])] + [("img", b) for b in image_bits[1:]]
    right = [("img", image_bits[0])] + [("img", b) for b in reversed(image_bits[1:])]
    whole_sum = width // devices >= 16
    if whole_sum:
        lane_steps = [("row", b) for b in bits_of(lanes)]
        left, right = left + lane_steps, right + lane_steps
    count = len(left)
    unit = width >> count
    sds = jax.ShapeDtypeStruct
    page = lambda n, kind=BF16: pltpu.VMEM((n, rows, width), kind)
    dma = lambda *shape: pltpu.SemaphoreType.DMA(shape)
    macs = rounds * (rows * width * width * 18 + rows * rows * width * 7)
    block_out, latents_grad, down_grad, up_grad, out_grad, qkv_grad, totals = pl.pallas_call(
        functools.partial(block_kernel, images, lanes, slots, left, right, whole_sum),
        out_shape=[sds(latents.shape, BF16)] * 2 + [sds((unit, width), F32)] * 3 + [sds((unit, 3 * width), F32), sds((8, width), F32)],
        in_specs=[SM] + [VM] * 7 + [ANY] * 6,
        out_specs=[ANY] * 2 + [VM] * 5,
        scratch_shapes=[
            pltpu.VMEM((width, 3 * width), BF16), pltpu.VMEM((width, width), BF16), pltpu.VMEM((width, width), BF16),
            pltpu.VMEM((width, width), BF16),
            page(rounds), page(rounds), page(rounds), page(3 * rounds), page(rounds, F32), page(6 + 3 * rounds),
            page(3 * rounds), page(1), page(rounds),
            pltpu.VMEM((rounds, HEADS // 4, rows, 128), F32),
            pltpu.VMEM((count + 1, 8, width), F32), pltpu.VMEM((count, 8, width), F32),
            page(3), page(3),
            dma(4), dma(4, rounds),
            dma(rounds, lanes), dma(rounds, lanes), dma(rounds, lanes), dma(rounds, lanes),
            dma(rounds, lanes), dma(rounds, lanes), dma(rounds, lanes), dma(rounds, lanes),
            dma(2, count, 2), dma(2, count, 2), pltpu.SemaphoreType.REGULAR((count, 2)), dma(count), dma(count),
        ],
        compiler_params=pltpu.CompilerParams(collective_id=0, has_side_effects=True, vmem_limit_bytes=VMEM_LIMIT),
        cost_estimate=pl.CostEstimate(flops=2 * macs, bytes_accessed=32 << 20, transcendentals=0),
        name="latent_block",
    )(slot_crops, ln1_scale, ln1_offset, ln2_scale, ln2_offset, out_bias, up_bias, down_bias, latents, cotangent, qkv_weight, out_weight, up_weight, down_weight)
    if not whole_sum:
        down_grad, up_grad, out_grad, qkv_grad = [
            lax.psum_scatter(g, "row", scatter_dimension=0, tiled=True) for g in (down_grad, up_grad, out_grad, qkv_grad)]
        totals = lax.psum(totals, "row")
    me = lax.axis_index("img") * lanes + lax.axis_index("row")
    part = width // devices
    mine = lax.dynamic_slice(totals, (0, me * part), (8, part))
    return (
        block_out, latents_grad, mine[5], mine[6], qkv_grad, out_grad, mine[4], mine[2], mine[3], up_grad, mine[1], down_grad,
        mine[0],
    )


def solution(mesh):
    whole, both = P(), P(("img", "row"))
    rows, wide = P("img", "row", None), P(("img", "row"), None)
    in_specs = (rows, rows, P("img")) + (whole,) * 11
    out_specs = (rows, rows, both, both, wide, wide, both, both, both, wide, both, wide, both)
    return jax.shard_map(local, mesh=mesh, in_specs=in_specs, out_specs=out_specs, check_vma=False)
```

profile of v0, /device:TPU:0, one launch (start us, length us, event | category | flops | bytes accessed | tf_op | source)
XLA Modules:
  0.0 217.2 jit_solution(5617151484294406417)
XLA Ops:
  0.7 207.9 %latent_block.1 = (bf16[8,128,1024]{2,1,0:T(8,128)(2,1)}, bf16[8,128,1024]{2,1,0:T(8,128)(2,1)}, f32[32,1024]{1,0:T(8,128)}, f32[32,1024]{1,0:T(8,128)}, f32[32,...) custom-call(s32[8]{0:T(128)} %refs_0_.1, bf16[1024]{0:T(1024)(128)(2,1)} %refs_1_.1, bf16[1024]{0:T(1024)(128)(2,1)} %refs_2_.1, ...), custom_call_target="tpu_custom_call" | custom-call | flops 46170898432 | bytes 33554432 | tf_op jit(solution)/shard_map/latent_block/pallas_call | solution.py:436
  208.6 0.8 constant_dynamic-slice_fusion
  209.3 0.5 slice_bitcast_fusion
  209.9 0.0 copy-start
  209.9 3.2 %copy.33 = bf16[8,128,1024]{2,1,0:T(8,128)(2,1)} copy(bf16[8,128,1024]{2,1,0:T(8,128)(2,1)} %get-tuple-element.47) | data formatting | bytes 4194304
  213.1 0.0 copy-done
  213.1 0.0 copy-start.1
  213.1 0.0 copy-start.4
  213.1 0.0 copy-start.3
  213.1 0.0 copy-start.2
  213.1 1.3 copy.34
  214.4 0.0 copy-done.1
  214.4 0.7 copy.35
  215.2 0.0 copy-done.4
  215.2 0.7 copy.36
  215.8 0.0 copy-done.3
  215.9 0.7 copy.37
  216.5 0.0 copy-done.2
  216.5 0.7 copy.38
Async XLA Ops:
  209.9 3.2 %copy-start = (bf16[8,128,1024]{2,1,0:T(8,128)(2,1)S(1)}, bf16[8,128,1024]{2,1,0:T(8,128)(2,1)}, u32[]{:S(2)}) copy-start(bf16[8,128,1024]{2,1,0:T(8,128)(2,1)} %get-tuple-element.48) | copy-start | bytes 6291460
  213.1 1.3 copy-start.1
  213.1 2.1 copy-start.4
  213.1 2.7 %copy-start.3 = (f32[32,1024]{1,0:T(8,128)S(1)}, f32[32,1024]{1,0:T(8,128)}, u32[]{:S(2)}) copy-start(f32[32,1024]{1,0:T(8,128)} %get-tuple-element.56) | copy-start | bytes 393220
  213.1 3.4 %copy-start.2 = (f32[32,1024]{1,0:T(8,128)S(1)}, f32[32,1024]{1,0:T(8,128)}, u32[]{:S(2)}) copy-start(f32[32,1024]{1,0:T(8,128)} %get-tuple-element.58) | copy-start | bytes 393220
where the time goes:
time: 217 us
  Pallas kernels  208 us (96%)
  local copies, waits for them, and re-layouts  8.58 us (4%)
    pallas_call x1, Pallas kernels, local(): pl.pallas_call(functools.partial(block_kernel, images, lanes, slots, left...  208 us
    unnamed x16, local copies, waits for them, and re-layouts  7.28 us

commit v1 on v0

--- a/solution.py
+++ b/solution.py
@@ -17,6 +17,7 @@
 GELU_A = 0.7978845608028654
 GELU_B = 0.044715
 LOG2_E = 1.4426950408889634
+EARLY = {1: (3, 2), 3: (1,)}
 VMEM_LIMIT = 64 * 1024 * 1024 - 64 * 1024
 
 
@@ -58,17 +59,15 @@
 def block_kernel(images, lanes, places, steps_left, steps_right, in_lanes, *refs):
     crops, vectors, (lat, cot), refs = refs[0], refs[1:8], refs[8:10], refs[10:]
     mats, refs = refs[:4], refs[4:]
-    (out_block, out_grad), refs = refs[:2], refs[2:]
-    mlp_out, (qkv_out, sums_out), refs = refs[:3], refs[3:5], refs[5:]
-    (vq, vo, vu, vd, xr, cr, h1, qkv, resid, work, back, gm, bo, lse, sums, sums_got, got_first, got_next), refs = refs[:18], refs[18:]
+    (results, products_out, sums_out), refs = refs[:3], refs[3:]
+    (vq, vo, vu, vd, xr, cr, h1, qkv, resid, summed, factors, back, gm, bo, lse, sums, sums_got, got_first, got_next), refs = refs[:19], refs[19:]
     (mat_sem, own_sem, lat_out, lat_in, cot_out, cot_in, bo_out, bo_in, lg_out, lg_in,
      red_out, red_in, credit, sum_out, sum_in) = refs
     rounds, rows, width = h1.shape
     chunk = rows // lanes
     size = width // HEADS
     img, z = lax.axis_index("img"), lax.axis_index("row")
-    left_pages, slope = 6, 0
-    act, h2, mixed = (left_pages + rounds * i for i in range(3))
+    act, h2, mixed = (rounds * i for i in range(3))
     gl, gp, ga = (rounds * i for i in range(3))
     last = rounds - 1
 
@@ -103,17 +102,18 @@
             src_ref=source.at[place(r, lane(k))], dst_ref=target.at[r, pl.ds(k * chunk, chunk)],
             send_sem=sent.at[r, k], recv_sem=got.at[r, k], device_id=(img, lane(k)), device_id_type=MESH)
 
-    def piece_out(source, target, sent, got, own, r, k):
+    def piece_out(source, first, sent, got, own, r, k):
+        target = results.at[first + place(r, z)]
         if k == 0:
-            return pltpu.make_async_copy(source.at[r, pl.ds(0, chunk)], target.at[place(r, z)], own_sem.at[own, r])
+            return pltpu.make_async_copy(source.at[r, pl.ds(0, chunk)], target, own_sem.at[own, r])
         return pltpu.make_async_remote_copy(
-            src_ref=source.at[r, pl.ds(k * chunk, chunk)], dst_ref=target.at[place(r, z)],
+            src_ref=source.at[r, pl.ds(k * chunk, chunk)], dst_ref=target,
             send_sem=sent.at[r, k], recv_sem=got.at[r, k], device_id=(img, lane(k)), device_id_type=MESH)
 
     lat_piece = functools.partial(piece_in, lat, xr, lat_out, lat_in, 0)
     cot_piece = functools.partial(piece_in, cot, cr, cot_out, cot_in, 1)
-    bo_piece = functools.partial(piece_out, bo, out_block, bo_out, bo_in, 2)
-    lg_piece = functools.partial(piece_out, xr, out_grad, lg_out, lg_in, 3)
+    bo_piece = functools.partial(piece_out, bo, 0, bo_out, bo_in, 2)
+    lg_piece = functools.partial(piece_out, xr, places, lg_out, lg_in, 3)
 
     def arrive(piece, r, k):
         move = piece(r, k)
@@ -133,6 +133,19 @@
 
     issue(lat_piece, 0)
 
+    def issue_next(piece, r, k):
+        for kk in EARLY.get(k, ()):
+            @pl.when(r < last)
+            def _():
+                piece(r + 1, kk).start()
+
+            @pl.when(r == last)
+            def _():
+                if piece is lat_piece:
+                    cot_piece(0, kk).start()
+                else:
+                    bo_piece(0, kk).start()
+
     half = rows // 2
     halves = [pl.ds(i * half, half) for i in range(2)]
     vector = lambda i: vectors[i][...].astype(F32).reshape(1, width)
@@ -147,14 +160,7 @@
             part = pl.ds(k * chunk, chunk)
             hat, _ = norm_parts(xr[r, part, :].astype(F32))
             h1[r, part, :] = (hat * s1 + o1).astype(BF16)
-
-        @pl.when(r < last)
-        def _():
-            issue(lat_piece, r + 1)
-
-        @pl.when(r == last)
-        def _():
-            issue(cot_piece, 0)
+            issue_next(lat_piece, r, k)
 
         for n in range(3):
             qkv[3 * r + n] = dot(h1[r], vq[:, n * width:(n + 1) * width]).astype(BF16)
@@ -170,26 +176,26 @@
                 e = jnp.exp2((s - top) * factor)
                 total = jnp.sum(e, 1, keepdims=True)
                 lse[r, group, :, i:i + 1] = top * factor + jnp.log2(total)
-                work[mixed + r, :, cols] = (dot(e.astype(BF16), v) * (1.0 / total)).astype(BF16)
+                factors[mixed + r, :, cols] = (dot(e.astype(BF16), v) * (1.0 / total)).astype(BF16)
 
         bo_, s2, o2 = vector(4), vector(2), vector(3)
         for part in halves:
-            value = xr[r, part, :].astype(F32) + dot(work[mixed + r, part, :], vo[...]) + bo_
+            value = xr[r, part, :].astype(F32) + dot(factors[mixed + r, part, :], vo[...]) + bo_
             resid[r, part, :] = value
             hat, _ = norm_parts(value)
-            work[h2 + r, part, :] = (hat * s2 + o2).astype(BF16)
+            factors[h2 + r, part, :] = (hat * s2 + o2).astype(BF16)
         bu = vector(5)
         for part in halves:
-            u = dot(work[h2 + r, part, :], vu[...]) + bu
+            u = dot(factors[h2 + r, part, :], vu[...]) + bu
             t = jnp.tanh(GELU_A * (u + GELU_B * u * u * u))
-            work[act + r, part, :] = (0.5 * u * (1.0 + t)).astype(BF16)
-            work[slope + r, part, :] = (
+            factors[act + r, part, :] = (0.5 * u * (1.0 + t)).astype(BF16)
+            back[gp + r, part, :] = (
                 0.5 * (1.0 + t) + 0.5 * u * (1.0 - t * t) * (GELU_A * (1.0 + 3.0 * GELU_B * u * u))
             ).astype(BF16)
         bd = vector(6)
         keep = jnp.minimum(crops[place(r, z)], 1).astype(F32)
         for part in halves:
-            value = resid[r, part, :] + dot(work[act + r, part, :], vd[...]) + bd
+            value = resid[r, part, :] + dot(factors[act + r, part, :], vd[...]) + bd
             bo[r, part, :] = (value * keep).astype(BF16)
         bo_piece(r, 0).start()
 
@@ -205,18 +211,15 @@
             g = (cr[r, part, :].astype(F32) * share).astype(BF16)
             back[gl + r, part, :] = g
             add_sum(0, column_sum(g.astype(F32)))
-
-        @pl.when(r < last)
-        def _():
-            issue(cot_piece, r + 1)
+            issue_next(cot_piece, r, k)
 
         @pl.when(r == last)
         def _():
-            for s in range(rounds):
+            for s in range(1, rounds):
                 issue(bo_piece, s)
 
         for part in halves:
-            g = (dot_t(back[gl + r, part, :], vd[...]) * work[slope + r, part, :].astype(F32)).astype(BF16)
+            g = (dot_t(back[gl + r, part, :], vd[...]) * back[gp + r, part, :].astype(F32)).astype(BF16)
             back[gp + r, part, :] = g
             add_sum(1, column_sum(g.astype(F32)))
         s2 = vector(2)
@@ -259,101 +262,110 @@
             add_sum(6, column_sum(gh))
             xr[r, part, :] = (resid[r, part, :] + norm_back(gh * s1, hat, inverse)).astype(BF16)
 
+    totals = (summed, factors)
     count = len(steps_left)
     unit = width >> count
     per_half = width // 2 // unit
     sides = (slice(0, width // 2), slice(width // 2, width))
 
-    def spot(block, steps):
-        found = 0
-        for axis, bit in steps:
+    def spots(steps):
+        terms = []
+        for i, (axis, bit) in enumerate(steps):
             mine = (img // bit) % 2 if axis == "img" else (z // bit) % 2
             scale = 1 if axis == "row" else (width // unit) // images
-            theirs = (block // (bit * scale)) % 2
-            found = found * 2 + (theirs + mine) % 2
+            weight = 1 if i == 0 else unit << (count - 1 - i)
+            terms.append((bit * scale, (mine * weight, (1 - mine) * weight)))
+        found = []
+        for block in range(width // unit):
+            picked = [pair[(block // divisor) % 2] for divisor, pair in terms]
+            found.append((picked[0], pl.multiple_of(sum(picked[2:], picked[1]), unit)))
         return found
 
-    def place_products(base, left, right):
+    def place_products(total_pages, rounds_of, left, right):
+        places_of = [spots(steps_left), spots(steps_right)]
+        first_round = rounds_of[0]
+
         @pl.loop(0, 3)
         def _(c):
-            for steps, offset in ((steps_left, 0), (steps_right, width // 2)):
+            for side, offset in ((0, 0), (1, width // 2)):
                 for first_column in range(offset, offset + width // 2, 256):
                     cols = slice(first_column, first_column + 256)
-                    total = dot_tt(left(c, 0), right(c, 0, cols))
-                    for r in range(1, rounds):
+                    total = dot_tt(left(c, first_round), right(c, first_round, cols))
+                    for r in rounds_of[1:]:
                         total = total + dot_tt(left(c, r), right(c, r, cols))
-                    total = total.astype(BF16)
-                    for block in range(width // unit):
-                        at = spot(block, steps)
-                        first = pl.multiple_of((at % per_half) * unit, unit)
-                        work[base + c + 3 * (at // per_half), pl.ds(first, unit), cols] = total[block * unit:(block + 1) * unit]
-
-    def send(base, group, step, side):
+                    for block, (goes, first) in enumerate(places_of[side]):
+                        rows_of = (c + 3 * goes, pl.ds(first, unit), cols)
+                        part = total[block * unit:(block + 1) * unit]
+                        if len(rounds_of) == 1:
+                            part = part + jnp.where(first_round > 0, total_pages[rows_of].astype(F32), 0.0)
+                        total_pages[rows_of] = part.astype(BF16)
+
+    def send(group, step, side):
         steps = (steps_left, steps_right)[side]
         if step == 0:
-            source, target = work.at[pl.ds(base + 3, 3)], got_first
+            source, target = totals[group].at[pl.ds(3, 3)], got_first
         else:
             length = rows >> step
-            source = work.at[pl.ds(base, 3), pl.ds(length, length), sides[side]]
+            source = totals[group].at[pl.ds(0, 3), pl.ds(length, length), sides[side]]
             target = got_next.at[:, pl.ds(rows - 2 * length, length), sides[side]]
         return pltpu.make_async_remote_copy(
             src_ref=source, dst_ref=target, send_sem=red_out.at[group, step, side], recv_sem=red_in.at[group, step, side],
             device_id=device(*steps[step]), device_id_type=MESH)
 
-    def begin(base, group, step, side):
+    def begin(group, step, side):
         if group:
             pl.semaphore_wait(credit.at[step, side], 1)
-        send(base, group, step, side).start()
-
-    def reduce_step(base, group, step):
+        send(group, step, side).start()
+
+    def reduce_step(group, step):
         length = rows >> step
         middle = length // 2
         for side in (0, 1):
             cols = sides[side]
             if step or side == 0:
-                send(base, group, step, side).wait_recv()
+                send(group, step, side).wait_recv()
 
             def added(c, first, extent):
                 if step == 0:
                     got = got_first[c, pl.ds(first, extent), cols]
                 else:
                     got = got_next[c, pl.ds(rows - 2 * length + first, extent), cols]
-                return work[base + c, pl.ds(first, extent), cols].astype(F32) + got.astype(F32)
+                return totals[group][c, pl.ds(first, extent), cols].astype(F32) + got.astype(F32)
 
             if step == count - 1:
                 for c in range(3):
-                    if group:
-                        qkv_out[:, c * width + cols.start:c * width + cols.stop] = added(c, 0, length)
-                    else:
-                        mlp_out[c][:, cols] = added(c, 0, length)
+                    first_column = (3 * group + c) * width
+                    products_out[:, first_column + cols.start:first_column + cols.stop] = added(c, 0, length)
             else:
                 def keep_part(first):
                     @pl.loop(0, 3)
                     def _(c):
-                        work[base + c, pl.ds(first, middle), cols] = added(c, first, middle).astype(BF16)
+                        totals[group][c, pl.ds(first, middle), cols] = added(c, first, middle).astype(BF16)
 
                 keep_part(middle)
-                begin(base, group, step + 1, side)
+                begin(group, step + 1, side)
                 keep_part(0)
             if group == 0 and (step or side):
                 steps = (steps_left, steps_right)[side]
                 pl.semaphore_signal(
                     credit.at[step, side if step else 0], inc=1, device_id=device(*steps[step]), device_id_type=MESH)
 
-    mlp_base, qkv_base = 0, left_pages
     for load in loads:
         load.wait()
     loop_rounds(forward)
 
+    def mlp_products(r):
+        place_products(
+            summed, [r], lambda c, s: factors[rounds * c + s], lambda c, s, cols: back[rounds * c + s, :, cols])
+
     @loop_rounds
     def _(r):
         backward_mlp(r)
 
         @pl.when(r == last)
         def _():
-            place_products(
-                mlp_base, lambda c, s: work[left_pages + rounds * c + s], lambda c, s, cols: back[rounds * c + s, :, cols])
-            begin(mlp_base, 0, 0, 0)
+            mlp_products(r)
+            begin(0, 0, 0)
 
         backward_attention(r)
 
@@ -361,12 +373,17 @@
         def _():
             for s in range(last):
                 issue(lg_piece, s)
-            reduce_step(mlp_base, 0, 0)
-            place_products(qkv_base, lambda c, s: h1[s], lambda c, s, cols: qkv[3 * s + c, :, cols])
-            begin(qkv_base, 1, 0, 0)
+            reduce_step(0, 0)
+            place_products(
+                factors, range(rounds), lambda c, s: h1[s], lambda c, s, cols: qkv[3 * s + c, :, cols])
+            begin(1, 0, 0)
 
         backward_input(r)
         lg_piece(r, 0).start()
+
+        @pl.when(r < last)
+        def _():
+            mlp_products(r)
 
 
     gates = {count - 3: [2], count - 2: [3], count - 1: [1]} if in_lanes and lanes == 4 else {0: range(1, lanes)}
@@ -385,10 +402,10 @@
     results_out(0)
     for step in range(1, count + 1):
         if step < count:
-            reduce_step(mlp_base, 0, step)
+            reduce_step(0, step)
         if step == count - 3:
             results_out(step)
-        reduce_step(qkv_base, 1, step - 1)
+        reduce_step(1, step - 1)
         if step > count - 3:
             results_out(step)
         sum_moves[step - 1].wait()
@@ -397,11 +414,11 @@
             sum_moves[step].start()
     sums_out[...] = sums[count]
 
-    for group, base in enumerate((mlp_base, qkv_base)):
-        send(base, group, 0, 0).wait_send()
+    for group in (0, 1):
+        send(group, 0, 0).wait_send()
         for step in range(1, count):
             for side in (0, 1):
-                send(base, group, step, side).wait_send()
+                send(group, step, side).wait_send()
     for r in range(rounds):
         for k in range(1, lanes):
             lat_piece(r, k).wait_send()
@@ -433,15 +450,15 @@
     page = lambda n, kind=BF16: pltpu.VMEM((n, rows, width), kind)
     dma = lambda *shape: pltpu.SemaphoreType.DMA(shape)
     macs = rounds * (rows * width * width * 18 + rows * rows * width * 7)
-    block_out, latents_grad, down_grad, up_grad, out_grad, qkv_grad, totals = pl.pallas_call(
+    results, products, totals = pl.pallas_call(
         functools.partial(block_kernel, images, lanes, slots, left, right, whole_sum),
-        out_shape=[sds(latents.shape, BF16)] * 2 + [sds((unit, width), F32)] * 3 + [sds((unit, 3 * width), F32), sds((8, width), F32)],
+        out_shape=[sds((2 * slots, chunk, width), BF16), sds((unit, 6 * width), F32), sds((8, width), F32)],
         in_specs=[SM] + [VM] * 7 + [ANY] * 6,
-        out_specs=[ANY] * 2 + [VM] * 5,
+        out_specs=[ANY] + [VM] * 2,
         scratch_shapes=[
             pltpu.VMEM((width, 3 * width), BF16), pltpu.VMEM((width, width), BF16), pltpu.VMEM((width, width), BF16),
             pltpu.VMEM((width, width), BF16),
-            page(rounds), page(rounds), page(rounds), page(3 * rounds), page(rounds, F32), page(6 + 3 * rounds),
+            page(rounds), page(rounds), page(rounds), page(3 * rounds), page(rounds, F32), page(6), page(max(6, 3 * rounds)),
             page(3 * rounds), page(1), page(rounds),
             pltpu.VMEM((rounds, HEADS // 4, rows, 128), F32),
             pltpu.VMEM((count + 1, 8, width), F32), pltpu.VMEM((count, 8, width), F32),
@@ -456,9 +473,10 @@
         name="latent_block",
     )(slot_crops, ln1_scale, ln1_offset, ln2_scale, ln2_offset, out_bias, up_bias, down_bias, latents, cotangent, qkv_weight, out_weight, up_weight, down_weight)
     if not whole_sum:
-        down_grad, up_grad, out_grad, qkv_grad = [
-            lax.psum_scatter(g, "row", scatter_dimension=0, tiled=True) for g in (down_grad, up_grad, out_grad, qkv_grad)]
+        products = lax.psum_scatter(products, "row", scatter_dimension=0, tiled=True)
         totals = lax.psum(totals, "row")
+    down_grad, up_grad, out_grad, qkv_grad = jnp.split(products, (width, 2 * width, 3 * width), 1)
+    block_out, latents_grad = results[:slots], results[slots:]
     me = lax.axis_index("img") * lanes + lax.axis_index("row")
     part = width // devices
     mine = lax.dynamic_slice(totals, (0, me * part), (8, part))

time: 217 us -> 216 us (level)
    unnamed x16 -> x2, local copies, waits for them, and re-layouts: 7.28 us -> 0.01 us
    slice x0 -> x1, local copies, waits for them, and re-layouts: none -> 4.91 us  [local(): block_out, latents_grad = (results[:slots], results[slots:])]
where the time goes in v1:
time: 216 us
  Pallas kernels  207 us (96%)
  local copies, waits for them, and re-layouts  7.72 us (4%)
    pallas_call x1, Pallas kernels, local(): pl.pallas_call(functools.partial(block_kernel, images, lanes, slots, left...  207 us
    slice x1, local copies, waits for them, and re-layouts, local(): block_out, latents_grad = (results[:slots], results[slots:])  4.91 us

profile of v1, /device:TPU:0, one launch (start us, length us, event | category | flops | bytes accessed | tf_op | source)
XLA Modules:
  0.0 215.7 jit_solution(6944102924104712323)
XLA Ops:
  0.7 207.3 %latent_block.1 = (bf16[16,128,1024]{2,1,0:T(8,128)(2,1)}, f32[32,6144]{1,0:T(8,128)}, f32[8,1024]{1,0:T(8,128)}) custom-call(s32[8]{0:T(128)} %refs_0_.1, bf16[1024]{0:T(1024)(128)(2,1)} %refs_1_.1, bf16[1024]{0:T(1024)(128)(2,1)} %refs_2_.1, bf16[1024]{0:T(1024)(128)(2,1)} %refs_3_.1, bf16[1024]{0:T(1024)(128)(2,1)} %refs_4_.1, bf16[1024]{0:T(1024)(128)(2,1)} %refs_5_.1, ...), custom_call_target="tpu_custom_call" | custom-call | flops 46170898432 | bytes 33554432 | tf_op jit(solution)/shard_map/latent_block/pallas_call | solution.py:453
  207.9 0.0 copy-start
  207.9 4.9 %fusion = (bf16[8,128,1024]{2,1,0:T(8,128)(2,1)}, bf16[8,128,1024]{2,1,0:T(8,128)(2,1)}) fusion(bf16[16,128,1024]{2,1,0:T(8,128)(2,1)} %get-tuple-element.16), kind=kLoop, calls=%fused_computation.8 | loop fusion | bytes 8388608 | tf_op jit(solution)/shard_map/slice | solution.py:479
  212.8 0.7 constant_dynamic-slice_fusion
  213.6 0.5 slice_bitcast_fusion
  214.1 0.0 copy-done
  214.1 0.8 split.12
  214.9 0.8 fusion.1
Async XLA Ops:
  207.9 6.2 %copy-start = (f32[32,6144]{1,0:T(8,128)S(1)}, f32[32,6144]{1,0:T(8,128)}, u32[]{:S(2)}) copy-start(f32[32,6144]{1,0:T(8,128)} %get-tuple-element.18) | copy-start | bytes 2359300

commit v2 on v1

--- a/solution.py
+++ b/solution.py
@@ -426,6 +426,20 @@
         for piece in (bo_piece, lg_piece):
             for k in range(lanes):
                 piece(r, k).wait()
+
+
+def finish_kernel(part, lanes, first, second, products, sums, block_out, latents_grad, down, up, out, qkv, mine):
+    block_out[...] = first[...]
+    latents_grad[...] = second[...]
+
+    @pl.when(pl.program_id(0) == 0)
+    def _():
+        width = down.shape[1]
+        for i, target in enumerate((down, up, out)):
+            target[...] = products[:, i * width:(i + 1) * width]
+        qkv[...] = products[:, 3 * width:]
+        start = (lax.axis_index("img") * lanes + lax.axis_index("row")) * part
+        mine[...] = pltpu.roll(sums[...], (width - start) % width, 1)[:, :128]
 
 
 def local(
@@ -475,11 +489,21 @@
     if not whole_sum:
         products = lax.psum_scatter(products, "row", scatter_dimension=0, tiled=True)
         totals = lax.psum(totals, "row")
-    down_grad, up_grad, out_grad, qkv_grad = jnp.split(products, (width, 2 * width, 3 * width), 1)
-    block_out, latents_grad = results[:slots], results[slots:]
-    me = lax.axis_index("img") * lanes + lax.axis_index("row")
     part = width // devices
-    mine = lax.dynamic_slice(totals, (0, me * part), (8, part))
+    steps = 2 if slots % 2 == 0 else 1
+    whole = lambda *shape: pl.BlockSpec(shape, lambda i: (0,) * len(shape))
+    some = lambda first: pl.BlockSpec((slots // steps, chunk, width), lambda i: (first + i, 0, 0))
+    share_rows = products.shape[0]
+    block_out, latents_grad, down_grad, up_grad, out_grad, qkv_grad, mine = pl.pallas_call(
+        functools.partial(finish_kernel, part, lanes),
+        grid=(steps,),
+        out_shape=[sds(latents.shape, BF16)] * 2 + [sds((share_rows, width), F32)] * 3
+        + [sds((share_rows, 3 * width), F32), sds((8, 128), F32)],
+        in_specs=[some(0), some(steps), whole(share_rows, 6 * width), whole(8, width)],
+        out_specs=[some(0), some(0)] + [whole(share_rows, width)] * 3 + [whole(share_rows, 3 * width), whole(8, 128)],
+        name="results_apart",
+    )(results, results, products, totals)
+    mine = mine[:, :part]
     return (
         block_out, latents_grad, mine[5], mine[6], qkv_grad, out_grad, mine[4], mine[2], mine[3], up_grad, mine[1], down_grad,
         mine[0],

time: 216 us -> 214 us (level)
  local copies, waits for them, and re-layouts: 7.72 us -> 1.47 us
  Pallas kernels: 207 us -> 212 us
    slice x1 -> x0, local copies, waits for them, and re-layouts: 4.91 us -> none  [local(): block_out, latents_grad = (results[:slots], results[slots:])]
    pallas_call x0 -> x1, Pallas kernels: none -> 4.28 us  [local(): pl.pallas_call(functools.partial(finish_kernel, part, lanes), grid=(steps...]
where the time goes in v2:
time: 214 us
  Pallas kernels  212 us (99%)
    pallas_call x1, Pallas kernels, local(): pl.pallas_call(functools.partial(block_kernel, images, lanes, slots, left...  207 us

profile of v2, /device:TPU:0, one launch (start us, length us, event | category | flops | bytes accessed | tf_op | source)
XLA Modules:
  0.0 213.7 jit_solution(7065312222363067411)
XLA Ops:
  0.7 207.3 %latent_block.1 = (bf16[16,128,1024]{2,1,0:T(8,128)(2,1)}, f32[32,6144]{1,0:T(8,128)}, f32[8,1024]{1,0:T(8,128)}) custom-call(s32[8]{0:T(128)} %refs_0_.1, bf16[1024]{0:T(1024)(128)(2,1)} %refs_1_.1, bf16[1024]{0:T(1024)(128)(2,1)} %refs_2_.1, bf16[1024]{0:T(1024)(128)(2,1)} %refs_3_.1, bf16[1024]{0:T(1024)(128)(2,1)} %refs_4_.1, bf16[1024]{0:T(1024)(128)(2,1)} %refs_5_.1, ...), custom_call_target="tpu_custom_call" | custom-call | flops 46170898432 | bytes 33554432 | tf_op jit(solution)/shard_map/latent_block/pallas_call | solution.py:467
  207.9 4.3 %results_apart.1 = (bf16[8,128,1024]{2,1,0:T(8,128)(2,1)}, bf16[8,128,1024]{2,1,0:T(8,128)(2,1)}, f32[32,1024]{1,0:T(8,128)}, f32[32,1024]{1,0:T(8,128)}, f32[32...) custom-call(bf16[16,128,1024]{2,1,0:T(8,128)(2,1)} %get-tuple-element.23.first.second, ...), custom_call_target="tpu_custom_call" | custom-call | tf_op jit(solution)/shard_map/results_apart/pallas_call | solution.py:497
  212.2 1.5 slice_bitcast_fusion

commit v3 on v2

--- a/solution.py
+++ b/solution.py
@@ -386,7 +386,7 @@
             mlp_products(r)
 
 
-    gates = {count - 3: [2], count - 2: [3], count - 1: [1]} if in_lanes and lanes == 4 else {0: range(1, lanes)}
+    gates = {count - 3: [2, 1], count - 2: [3]} if in_lanes and lanes == 4 else {0: range(1, lanes)}
 
     def results_out(step):
         for k in gates.get(step, ()):

time: 214 us -> 214 us (level)
  no operation moved by 1% of the time
where the time goes in v3:
time: 214 us
  Pallas kernels  212 us (99%)
    pallas_call x1, Pallas kernels, local(): pl.pallas_call(functools.partial(block_kernel, images, lanes, slots, left...  208 us

profile of v3, /device:TPU:0, one launch (start us, length us, event | category | flops | bytes accessed | tf_op | source)
XLA Modules:
  0.0 214.0 jit_solution(12454227207092729049)
XLA Ops:
  0.7 207.6 %latent_block.1 = (bf16[16,128,1024]{2,1,0:T(8,128)(2,1)}, f32[32,6144]{1,0:T(8,128)}, f32[8,1024]{1,0:T(8,128)}) custom-call(s32[8]{0:T(128)} %refs_0_.1, bf16[1024]{0:T(1024)(128)(2,1)} %refs_1_.1, bf16[1024]{0:T(1024)(128)(2,1)} %refs_2_.1, bf16[1024]{0:T(1024)(128)(2,1)} %refs_3_.1, bf16[1024]{0:T(1024)(128)(2,1)} %refs_4_.1, bf16[1024]{0:T(1024)(128)(2,1)} %refs_5_.1, ...), custom_call_target="tpu_custom_call" | custom-call | flops 46170898432 | bytes 33554432 | tf_op jit(solution)/shard_map/latent_block/pallas_call | solution.py:467
  208.3 4.3 %results_apart.1 = (bf16[8,128,1024]{2,1,0:T(8,128)(2,1)}, bf16[8,128,1024]{2,1,0:T(8,128)(2,1)}, f32[32,1024]{1,0:T(8,128)}, f32[32,1024]{1,0:T(8,128)}, f32[32...) custom-call(bf16[16,128,1024]{2,1,0:T(8,128)(2,1)} %get-tuple-element.23.first.second, ...), custom_call_target="tpu_custom_call" | custom-call | tf_op jit(solution)/shard_map/results_apart/pallas_call | solution.py:497
  212.6 1.5 slice_bitcast_fusion
